TPU v7x, 256 devices: a whole 4x4x8 slice. The times are simulated.
256 devices in a mesh: dp: 2 (over z_lo), fsdp: 8 (over x, core), ctx: 16 (over y, z_hi).
Axes of the slice: x: 4, y: 4, z: 8 (z_hi: 4, z_lo: 2; z = z_hi * 2 + z_lo), core: 2. Of those that a mesh axis runs over, the one named last changes fastest.
Arguments:
- queries: bfloat16 [16, 2048, 1792], P(('dp', 'fsdp'), 'ctx'), may hold values from -56 to 56
- key_states: bfloat16 [16, 2048, 256], P(('dp', 'fsdp'), 'ctx'), may hold values from -16 to 16
- value_states: bfloat16 [16, 2048, 256], P(('dp', 'fsdp'), 'ctx'), may hold values from -6 to 6
- out_grad: bfloat16 [16, 2048, 1792], P(('dp', 'fsdp'), 'ctx'), may hold values from -6 to 6
- layer_input: bfloat16 [16, 2048, 3584], P(('dp', 'fsdp'), 'ctx'), may hold values from -6 to 6
- segment_ids: int32 [16, 2048], P(('dp', 'fsdp')), may hold values from 0 to 2, never falling along the last dimension, each value on 1 to 1536 neighbouring positions
Outputs:
- query_grad: bfloat16 [16, 2048, 1792], P(('dp', 'fsdp'), 'ctx')
- key_grad: bfloat16 [16, 2048, 256], P(('dp', 'fsdp'), 'ctx')
- value_grad: bfloat16 [16, 2048, 256], P(('dp', 'fsdp'), 'ctx')
- weight_grad: float32 [3584, 512], P('fsdp')
All inputs are finite; a program needn't handle non-finite values.
Results may differ from a plain program's by a relative error of at most 0.025.
Values may be sent and summed in bfloat16 or wider, within the bound.
No kernel may reach another device: no remote copies, remote signals or barrier semaphores. Data moves between devices by JAX's collectives and lax.ppermute only.
A program may use at most 128 MiB of HBM per device.

v0:
```python
import jax
import jax.numpy as jnp
from jax import lax
from jax.sharding import PartitionSpec as P

HD = 128


def group_forward(group_queries, all_keys, all_values, group_out, visible, softmax_scale):
    scores = (
        jnp.einsum("tpd,kd->tpk", group_queries, all_keys, preferred_element_type=jnp.float32)
        * softmax_scale
    )
    scores = jnp.where(visible[:, None, :], scores, -jnp.inf)
    row_max = jnp.max(scores, axis=-1, keepdims=True)
    shifted = jnp.exp(scores - row_max)
    weights = shifted / jnp.sum(shifted, axis=-1, keepdims=True)
    weights_low = weights.astype(jnp.bfloat16)
    outputs = jnp.einsum("tpk,kd->tpd", weights_low, all_values, preferred_element_type=jnp.float32)
    deltas = jnp.sum(group_out.astype(jnp.float32) * outputs, axis=-1, keepdims=True)
    prob_grad = jnp.einsum("tpd,kd->tpk", group_out, all_values, preferred_element_type=jnp.float32)
    score_grad = (weights * (prob_grad - deltas) * softmax_scale).astype(jnp.bfloat16)
    query_part = jnp.einsum("tpk,kd->tpd", score_grad, all_keys, preferred_element_type=jnp.float32)
    return (query_part, weights_low, score_grad)


def on_device(queries, key_states, value_states, out_grad, layer_input, segment_ids):
    local_rows = queries.shape[1]
    kv_width = key_states.shape[2]
    groups = kv_width // HD
    group_size = queries.shape[2] // kv_width
    softmax_scale = HD ** (-0.5)
    all_keys, all_values = (
        lax.all_gather(key_states[0], "ctx", axis=0, tiled=True),
        lax.all_gather(value_states[0], "ctx", axis=0, tiled=True),
    )
    length = all_keys.shape[0]
    offset = lax.axis_index("ctx") * local_rows
    positions = jnp.arange(length, dtype=jnp.int32)
    own_positions = offset + jnp.arange(local_rows, dtype=jnp.int32)
    segments = segment_ids[0]
    own_segments = lax.dynamic_slice_in_dim(segments, offset, local_rows)
    visible = (own_segments[:, None] == segments[None, :]) & (
        positions[None, :] <= own_positions[:, None]
    )
    local_queries = queries[0]
    local_out = out_grad[0]
    query_parts = []
    weight_blocks = []
    grad_blocks = []
    query_groups = []
    outgrad_groups = []
    for group in range(groups):
        left = group * group_size * HD
        right = (group + 1) * group_size * HD
        group_queries = local_queries[:, left:right].reshape(local_rows, group_size, HD)
        group_out = local_out[:, left:right].reshape(local_rows, group_size, HD)
        group_keys = all_keys[:, group * HD : (group + 1) * HD]
        group_values = all_values[:, group * HD : (group + 1) * HD]
        query_part, weights_low, score_grad = group_forward(
            group_queries, group_keys, group_values, group_out, visible, softmax_scale
        )
        query_parts.append(query_part.reshape(local_rows, group_size * HD))
        weight_blocks.append(weights_low)
        grad_blocks.append(score_grad)
        query_groups.append(group_queries)
        outgrad_groups.append(group_out)
    query_grad = jnp.concatenate(query_parts, axis=1).astype(jnp.bfloat16)
    key_cols = []
    value_cols = []
    for group in range(groups):
        grad_slice = grad_blocks[group]
        weight_slice = weight_blocks[group]
        key_cols.append(
            jnp.einsum(
                "tpk,tpd->kd", grad_slice, query_groups[group], preferred_element_type=jnp.float32
            )
        )
        value_cols.append(
            jnp.einsum(
                "tpk,tpd->kd",
                weight_slice,
                outgrad_groups[group],
                preferred_element_type=jnp.float32,
            )
        )
    kv_grad = lax.psum_scatter(
        jnp.concatenate(key_cols + value_cols, axis=1).astype(jnp.bfloat16),
        "ctx",
        scatter_dimension=0,
        tiled=True,
    )
    key_grad = kv_grad[:, :kv_width]
    value_grad = kv_grad[:, kv_width:]
    inputs = layer_input[0]
    token_count = local_rows * lax.axis_size("dp") * lax.axis_size("fsdp") * lax.axis_size("ctx")
    shares = lax.psum_scatter(
        jnp.einsum("td,tc->dc", inputs, kv_grad, preferred_element_type=jnp.float32),
        ("fsdp", "ctx"),
        scatter_dimension=0,
        tiled=True,
    )
    shares = lax.psum(shares.astype(jnp.bfloat16), "dp").astype(jnp.float32)
    totals = lax.all_gather(shares.astype(jnp.bfloat16), "ctx", axis=0, tiled=True).astype(
        shares.dtype
    )
    weight_grad = totals * token_count ** (-0.5)
    return (query_grad[None], key_grad[None], value_grad[None], weight_grad)


def solution(mesh):
    in_specs = (
        P(("dp", "fsdp"), "ctx", None),
        P(("dp", "fsdp"), "ctx", None),
        P(("dp", "fsdp"), "ctx", None),
        P(("dp", "fsdp"), "ctx", None),
        P(("dp", "fsdp"), "ctx", None),
        P(("dp", "fsdp"), None),
    )
    out_specs = (
        P(("dp", "fsdp"), "ctx", None),
        P(("dp", "fsdp"), "ctx", None),
        P(("dp", "fsdp"), "ctx", None),
        P("fsdp", None),
    )
    return jax.shard_map(
        on_device, mesh=mesh, in_specs=in_specs, out_specs=out_specs, check_vma=False
    )
```

profile of v0, /device:TPU:32, one launch (start us, length us, event | category | flops | bytes accessed | tf_op | source)
XLA Modules:
  0.0 1114.5 jit_solution(238175978882629624)
XLA Ops:
  7.2 0.0 copy-start
  7.2 0.0 all-gather.6.cloned.1.call-start
  7.2 0.7 all-gather.6.cloned.1.call-update
  7.9 0.0 all-gather.8.cloned.1.call-start
  8.0 0.7 all-gather.8.cloned.1.call-update
  8.7 0.0 reduce-scatter.5.cloned.1.call-start
  8.7 1.3 copy.39
  10.0 0.7 dynamic-slice_bitcast_fusion
  10.7 1.1 fusion.18
  11.8 0.0 copy-start.7
  11.8 1.3 copy.41
  13.2 51.6 %all-gather.6.cloned.1.call-done = bf16[1,2048,256]{2,1,0:T(8,128)(2,1)} async-done(((bf16[1,128,256]{2,1,0:T(8,128)(2,1)}), bf16[1,2048,256]{2,1,0:T(8,128)(2,1)}) %all-gather.6.cloned.1.call-update) | async-done | bytes 1048592 | tf_op jit(solution)/shard_map/all_gather | solution.py:34
  64.8 6.6 fusion.33
  71.5 0.0 copy-done.7
  71.5 4.2 fusion.11
  75.7 0.0 copy-start.1
  75.7 1.9 copy-done.1
  77.6 0.7 fusion.15
  78.3 39.8 %all-gather.8.cloned.1.call-done = bf16[1,2048,256]{2,1,0:T(8,128)(2,1)} async-done(((bf16[1,128,256]{2,1,0:T(8,128)(2,1)}), bf16[1,2048,256]{2,1,0:T(8,128)(2,1)}) %all-gather.8.cloned.1.call-update) | async-done | bytes 1048592 | tf_op jit(solution)/shard_map/all_gather | solution.py:35
  118.1 3.4 fusion.17
  121.5 0.0 copy-done.4
  121.5 6.6 fusion.34
  128.1 4.3 fusion.10
  132.4 0.0 copy-done.6
  132.4 1.2 fusion.16
  133.6 0.0 slice-start
  133.6 0.7 fusion.14
  134.3 0.0 slice-start.1
  134.3 5.3 multiply_convert_fusion
  139.6 0.0 copy-start.2
  139.6 0.8 fusion.13
  140.4 0.0 slice-done
  140.4 0.0 slice-done.1
  140.4 1.8 multiply_convert_fusion.1
  142.2 0.0 copy-done.2
  142.2 0.0 copy-start.3
  142.2 0.8 fusion.12
  143.0 1.1 copy-done.3
  144.0 0.2 pad_maximum_fusion
  144.2 0.0 copy-start.8
  144.2 2.6 copy.66
  146.8 0.0 reduce-scatter.5.cloned.1.call-update
  146.8 0.0 copy-done.8
  146.8 0.6 dynamic-slice.1
  148.1 3.4 convolution_convert_fusion
  151.4 0.2 copy.50
  151.6 3.3 convolution_convert_fusion.1
  154.9 0.2 copy.49
  155.0 0.8 pad_maximum_fusion.1
  155.8 77.6 %reduce-scatter.5.cloned.1.call-done = bf16[128,512]{1,0:T(8,128)(2,1)} async-done(((bf16[2048,512]{1,0:T(8,128)(2,1)}), bf16[128,512]{1,0:T(8,128)(2,1)}) %reduce-scatter.5.cloned.1.call-update) | async-done | bytes 131088
  233.5 0.9 fusion.32
  234.4 0.1 copy.71
  234.5 0.7 copy.53
  235.2 0.1 copy.70
  235.3 0.7 copy.52
  236.1 0.0 copy-done
  236.1 5.0 convolution_bitcast_fusion
  241.1 807.5 %all-reduce.2 = bf16[3584,512]{0,1:T(8,128)(2,1)} all-reduce(f32[3584,512]{0,1:T(8,128)} %convolution_bitcast_fusion), channel_id=5, replica_groups=mesh['dp'=2,'fsdp'=8,'ctx'=16] {'fsdp','ctx'}, use_global_device_ids=true, to_apply=%region_7.8.clone | all-reduce | flops 1835008 | bytes 11010048
  1048.5 1.1 dynamic-slice_convert_fusion
  1049.6 16.3 %psum.7 = bf16[28,512]{0,1:T(8,128)(2,1)S(1)} all-reduce(bf16[28,512]{0,1:T(8,128)(2,1)S(1)} %dynamic-slice_convert_fusion), channel_id=1, replica_groups=mesh['dp'=2,'fsdp'=8,'ctx'=16] {'dp'}, use_global_device_ids=true, to_apply=%region_8.9 | all-reduce | flops 14336 | bytes 57344 | tf_op jit(solution)/shard_map/psum | solution.py:103
  1065.9 0.1 copy.51
  1066.0 40.8 %all-gather.2 = bf16[16,28,512]{2,1,0:T(8,128)(2,1)S(1)} all-gather(bf16[1,28,512]{2,1,0:T(8,128)(2,1)S(1)} %copy.51), channel_id=1, replica_groups=mesh['dp'=2,'fsdp'=8,'ctx'=16] {'ctx'}, dimensions={0}, use_global_device_ids=true | all-gather | bytes 487424 | tf_op jit(solution)/shard_map/all_gather | solution.py:104
  1106.8 0.1 convert_multiply_fusion
  1106.9 1.0 reshape.122
  (8 shorter events, 0.1 us)
Async XLA Ops:
  7.2 228.9 %copy-start = (bf16[1,128,3584]{2,1,0:T(8,128)(2,1)S(1)}, bf16[1,128,3584]{2,1,0:T(8,128)(2,1)}, u32[]{:S(2)}) copy-start(bf16[1,128,3584]{2,1,0:T(8,128)(2,1)} %param.10) | copy-start | bytes 2752516
  7.2 57.7 %all-gather.6.cloned.1.call-start = ((), (), s32[]{:S(2)}) async-start(), calls=%async_computation.1 | async-start | bytes 1114112 | tf_op jit(solution)/shard_map/all_gather | solution.py:34
  7.9 110.2 %all-gather.8.cloned.1.call-start = ((), (), s32[]{:S(2)}) async-start(), calls=%async_computation.2 | async-start | bytes 1114112 | tf_op jit(solution)/shard_map/all_gather | solution.py:35
  8.7 224.8 %reduce-scatter.5.cloned.1.call-start = ((), (), s32[]{:S(2)}) async-start(), calls=%async_computation.3 | async-start | bytes 2228224
  11.8 59.7 %copy-start.7 = (pred[128,2048]{1,0:T(8,128)(4,1)}, pred[128,2048]{1,0:T(8,128)(4,1)S(1)}, u32[]{:S(2)}) copy-start(pred[128,2048]{1,0:T(8,128)(4,1)S(1)} %fusion.18) | copy-start | bytes 786436
  75.7 1.9 copy-start.1
  77.6 43.9 %copy-start.4 = (bf16[1,2048,256]{2,1,0:T(8,128)(2,1)S(1)}, bf16[1,2048,256]{2,1,0:T(8,128)(2,1)}, u32[]{:S(2)}) copy-start(bf16[1,2048,256]{2,1,0:T(8,128)(2,1)} %all-gather.6.cloned.1.call-done) | copy-start | bytes 3145732
  128.1 4.3 copy-start.6
  133.6 6.8 slice-start
  134.3 6.1 slice-start.1
  139.6 2.6 copy-start.2
  142.2 1.8 copy-start.3
  144.2 2.6 copy-start.8
  146.8 4.8 copy-start.5
Sparse Core Ops, SparseCore 0:
  10.4 54.3 all-gather.5
  67.3 50.7 all-gather.7
  146.9 86.4 reduce-scatter.4
where the time goes:
time: 1120 us; the launch traced here: 1110 us
  blocking collectives  865 us (77%)
  waiting for transfers between devices  170 us (15%)
  matrix products  39.4 us (4%)
  between operations  14.7 us (1%)
  local copies, waits for them, and re-layouts  14.6 us (1%)
    unnamed x1, blocking collectives  807 us
    unnamed x4, waiting for transfers between devices  79 us
    all_gather x1, waiting for transfers between devices, on_device(): lax.all_gather(key_states[0], 'ctx', axis=0, tiled=True)  51.6 us
    all_gather x1, blocking collectives, on_device(): lax.all_gather(shares.astype(jnp.bfloat16), 'ctx', axis=0, tiled=True)  40.8 us
    all_gather x1, waiting for transfers between devices, on_device(): lax.all_gather(value_states[0], 'ctx', axis=0, tiled=True)  39.8 us
  transfers between devices with their start and end apart: 3, of which 3 were waited for; matrix products, arithmetic and copies ran while one was open for 2% of the time, Pallas kernels for 0%

commit v1 on v0

v1 whole, which is shorter than its diff:
```python
import jax
import jax.numpy as jnp
from jax import lax
from jax.experimental import pallas as pl
from jax.experimental.pallas import tpu as pltpu
from jax.sharding import Mesh, PartitionSpec as P

HD = 128
GROUPS = 2
GS = 7
BLK = 128
KT = 256
LOG2E = 1.4426950408889634
SCALE = HD ** (-0.5)

DP, FX, FC, YH, YL, Z = "dp", "fx", "fc", "yh", "yl", "zh"
FSDP = (FX, FC)
YAX = (YH, YL)
CTX = (YH, YL, Z)
PARTNER = [(0, 3), (3, 0), (1, 2), (2, 1)]
NEIGHBOUR = [(0, 1), (1, 0), (2, 3), (3, 2)]


def attention_kernel(
    sc_ref, seg_ref, own_ref, recv_ref, kv_ref,
    dq_own_ref, dq_recv_ref, mine_ref, theirs_ref,
    s_ref, dp_ref, kt_ref, acc_ref, dqt_ref,
):
    length = kv_ref.shape[0]
    tiles = length // KT
    rows = GS * BLK
    nt = (((1,), (1,)), ((), ()))
    nn = (((1,), (0,)), ((), ()))
    f32 = jnp.float32
    bf16 = jnp.bfloat16
    seg = seg_ref[...]
    first = jnp.sum((seg < 1).astype(f32)).astype(jnp.int32)
    second = jnp.sum((seg < 2).astype(f32)).astype(jnp.int32)
    for t in range(tiles):
        kt_ref[t] = kv_ref[t * KT:(t + 1) * KT, 0:HD].T
    acc_ref[...] = jnp.zeros_like(acc_ref)

    def stack(ref, at):
        return jnp.concatenate(
            [ref[at * BLK:(at + 1) * BLK, h * HD:(h + 1) * HD] for h in range(GS)], axis=0
        )

    def block(src_ref, dq_ref, p0):
        qs = stack(src_ref, 0)
        dos = stack(src_ref, 1)
        qpos = p0 + lax.broadcasted_iota(jnp.int32, (1, BLK), 1)
        start = jnp.where(qpos >= second, second, jnp.where(qpos >= first, first, 0))
        low = jnp.where(p0 >= second, second, jnp.where(p0 >= first, first, 0))
        lo = low // KT
        hi = p0 // KT + 1

        def score(t, m):
            at = pl.multiple_of(t * KT, KT)
            k = kv_ref[pl.ds(at, KT), 0:HD]
            s = lax.dot_general(k, qs, nt, preferred_element_type=f32)
            kpos = at + lax.broadcasted_iota(jnp.int32, (KT, BLK), 0)
            seen = (kpos >= start) & (kpos <= qpos)
            s = jnp.concatenate(
                [jnp.where(seen, s[:, h * BLK:(h + 1) * BLK], -jnp.inf) for h in range(GS)], axis=1
            )
            s_ref[pl.ds(at, KT), :] = s
            return jnp.maximum(m, jnp.max(s, axis=0, keepdims=True))

        m = lax.fori_loop(lo, hi, score, jnp.full((1, rows), -jnp.inf, f32))

        def soft(t, carry):
            total, dot = carry
            at = pl.multiple_of(t * KT, KT)
            p = jnp.exp2((s_ref[pl.ds(at, KT), :] - m) * (SCALE * LOG2E))
            v = kv_ref[pl.ds(at, KT), HD:2 * HD]
            dp = lax.dot_general(v, dos, nt, preferred_element_type=f32)
            s_ref[pl.ds(at, KT), :] = p
            dp_ref[pl.ds(at, KT), :] = dp
            total = total + jnp.sum(p, axis=0, keepdims=True)
            dot = dot + jnp.sum(p * dp, axis=0, keepdims=True)
            return total, dot

        zero = jnp.zeros((1, rows), f32)
        total, dot = lax.fori_loop(lo, hi, soft, (zero, zero))
        inv = 1.0 / total
        delta = dot * inv
        inv_scaled = inv * SCALE
        dqt_ref[...] = jnp.zeros_like(dqt_ref)

        def grads(t, carry):
            at = pl.multiple_of(t * KT, KT)
            p = s_ref[pl.ds(at, KT), :]
            w = (p * inv).astype(bf16)
            ds = (p * (dp_ref[pl.ds(at, KT), :] - delta) * inv_scaled).astype(bf16)
            acc_ref[pl.ds(at, KT), 0:HD] += lax.dot_general(ds, qs, nn, preferred_element_type=f32)
            acc_ref[pl.ds(at, KT), HD:2 * HD] += lax.dot_general(
                w, dos, nn, preferred_element_type=f32
            )
            dqt_ref[...] += lax.dot_general(kt_ref[t], ds, nn, preferred_element_type=f32)
            return carry

        lax.fori_loop(lo, hi, grads, 0)
        for h in range(GS):
            dq_ref[:, h * HD:(h + 1) * HD] = dqt_ref[:, h * BLK:(h + 1) * BLK].T.astype(bf16)

    block(own_ref, dq_own_ref, sc_ref[0])
    block(recv_ref, dq_recv_ref, sc_ref[1])
    part = length // 4
    for j in range(2):
        for z in range(4):
            at = pl.multiple_of(sc_ref[2 + j] * part + z * BLK, BLK)
            mine_ref[z, j] = acc_ref[pl.ds(at, BLK), :]
            at = pl.multiple_of(sc_ref[4 + j] * part + z * BLK, BLK)
            theirs_ref[z, j] = acc_ref[pl.ds(at, BLK), :].astype(bf16)


def attention(scalars, seg, own, recv, kv):
    length = kv.shape[0]
    rows = GS * BLK
    vmem = pl.BlockSpec(memory_space=pltpu.VMEM)
    return pl.pallas_call(
        attention_kernel,
        out_shape=(
            jax.ShapeDtypeStruct((BLK, rows), jnp.bfloat16),
            jax.ShapeDtypeStruct((BLK, rows), jnp.bfloat16),
            jax.ShapeDtypeStruct((4, 2, BLK, 2 * HD), jnp.float32),
            jax.ShapeDtypeStruct((4, 2, BLK, 2 * HD), jnp.bfloat16),
        ),
        in_specs=[pl.BlockSpec(memory_space=pltpu.SMEM), vmem, vmem, vmem, vmem],
        out_specs=(vmem, vmem, vmem, vmem),
        scratch_shapes=[
            pltpu.VMEM((length, rows), jnp.float32),
            pltpu.VMEM((length, rows), jnp.float32),
            pltpu.VMEM((length // KT, HD, KT), jnp.bfloat16),
            pltpu.VMEM((length, 2 * HD), jnp.float32),
            pltpu.VMEM((HD, rows), jnp.float32),
        ],
        compiler_params=pltpu.CompilerParams(vmem_limit_bytes=48 * 1024 * 1024),
        cost_estimate=pl.CostEstimate(
            flops=5_000_000_000, bytes_accessed=8_000_000, transcendentals=4_000_000
        ),
    )(scalars, seg, own, recv, kv)


def on_device(queries, key_states, value_states, out_grad, layer_input, segment_ids):
    f32 = jnp.float32
    bf16 = jnp.bfloat16
    y = lax.axis_index(YAX)
    z = lax.axis_index(Z)
    g = lax.axis_index(YH)
    half = GS * HD
    k, v = key_states[0], value_states[0]
    kv_groups = [
        jnp.concatenate([k[:, i * HD:(i + 1) * HD], v[:, i * HD:(i + 1) * HD]], axis=1)
        for i in range(GROUPS)
    ]
    to_send = jnp.concatenate(
        [jnp.broadcast_to(x[None], (8, BLK, 2 * HD)) for x in kv_groups], axis=0
    )
    kv = lax.all_to_all(to_send, CTX, 0, 0).reshape(16 * BLK, 2 * HD)

    def halves(at):
        return jnp.concatenate(
            [
                lax.dynamic_slice_in_dim(queries[0], at, half, 1),
                lax.dynamic_slice_in_dim(out_grad[0], at, half, 1),
            ],
            axis=0,
        )

    recv = lax.ppermute(halves((1 - g) * half), YAX, PARTNER)
    own = halves(g * half)

    features = layer_input.shape[2] // 8
    x_out = layer_input[0].reshape(BLK, 8, features).transpose(1, 0, 2)
    x_own = lax.all_to_all(x_out, FSDP, 0, 0)
    x_recv = lax.ppermute(x_own, YAX, PARTNER)

    middle = ((y == 1) | (y == 2)).astype(jnp.int32)
    scalars = jnp.stack(
        [
            (y * 4 + z) * BLK,
            ((3 - y) * 4 + z) * BLK,
            middle,
            3 - middle,
            1 - middle,
            2 + middle,
        ]
    ).astype(jnp.int32)
    dq_own, dq_recv, mine, theirs = attention(
        scalars, segment_ids.reshape(16, 128), own, recv, kv
    )
    dq_other = lax.ppermute(dq_recv, YAX, PARTNER)
    query_grad = jnp.where(
        g == 0,
        jnp.concatenate([dq_own, dq_other], axis=1),
        jnp.concatenate([dq_other, dq_own], axis=1),
    )

    from_neighbour = lax.ppermute(theirs, YAX, NEIGHBOUR)
    partial = (mine + from_neighbour.astype(f32)).astype(bf16)
    shares = lax.all_to_all(partial, Z, 0, 0)
    kv_grad = jnp.sum(shares.astype(f32), axis=0).astype(bf16)
    grad_own = lax.dynamic_index_in_dim(kv_grad, g, 0, keepdims=False)
    grad_partner = lax.dynamic_index_in_dim(kv_grad, 1 - g, 0, keepdims=False)
    grad_other = lax.ppermute(grad_partner, YAX, PARTNER)
    grads = [jnp.where(g == 0, grad_own, grad_other), jnp.where(g == 0, grad_other, grad_own)]
    key_grad = jnp.concatenate([x[:, :HD] for x in grads], axis=1)
    value_grad = jnp.concatenate([x[:, HD:] for x in grads], axis=1)

    both = jnp.stack([grad_own, grad_partner])
    gathered = lax.all_to_all(jnp.broadcast_to(both[None], (8,) + both.shape), FSDP, 0, 0)
    part = jnp.einsum("ftd,ftc->dc", x_own, gathered[:, 0], preferred_element_type=f32)
    part = part + jnp.einsum("ftd,ftc->dc", x_recv, gathered[:, 1], preferred_element_type=f32)
    pieces = part.astype(bf16).reshape(16, features // 16, 2 * HD)
    pieces = lax.all_to_all(pieces, (DP, YL, Z), 0, 0)
    tokens = BLK * 256
    piece = (jnp.sum(pieces.astype(f32), axis=0) * tokens ** (-0.5)).astype(bf16)
    whole = lax.all_to_all(jnp.broadcast_to(piece[None], (32,) + piece.shape), (DP, YH, YL, Z), 0, 0)
    whole = whole.reshape(2, 2, 8, features // 16, 2, HD).transpose(0, 2, 3, 4, 1, 5)
    weight_grad = whole.reshape(features, 4 * HD).astype(f32)
    return (query_grad[None], key_grad[None], value_grad[None], weight_grad)


def solution(mesh):
    devices = mesh.devices.reshape(2, 4, 2, 2, 2, 4)
    fine = Mesh(devices, (DP, FX, FC, YH, YL, Z))
    rows = (DP, FX, FC)
    in_specs = (
        P(rows, CTX, None),
        P(rows, CTX, None),
        P(rows, CTX, None),
        P(rows, CTX, None),
        P(rows, CTX, None),
        P(rows, None),
    )
    out_specs = (
        P(rows, CTX, None),
        P(rows, CTX, None),
        P(rows, CTX, None),
        P((FX, FC), None),
    )
    return jax.shard_map(
        on_device, mesh=fine, in_specs=in_specs, out_specs=out_specs, check_vma=False
    )
```

time: 1120 us -> 175 us (0.16)
  blocking collectives: 865 us -> 0 us
  waiting for transfers between devices: 170 us -> 109 us
  starting transfers between devices: 0.11 us -> 40.2 us
  matrix products: 39.4 us -> 1.99 us
  between operations: 14.7 us -> 0.86 us
    unnamed x1 -> x0, blocking collectives: 807 us -> none
    all_gather x2 -> x0, waiting for transfers between devices: 91.4 us -> none  [the longest x1 51.6 us: on_device(): lax.all_gather(key_states[0], 'ctx', axis=0, tiled=True)]
    unnamed x4 -> x0, waiting for transfers between devices: 79 us -> none
    all_to_all x0 -> x6, waiting for transfers between devices: none -> 63.1 us  [the longest x1 14.8 us: on_device(): shares = lax.all_to_all(partial, Z, 0, 0)]
    ppermute x0 -> x5, waiting for transfers between devices: none -> 46 us  [the longest x1 19.6 us: on_device(): recv = lax.ppermute(halves((1 - g) * half), YAX, PARTNER)]
    all_gather x1 -> x0, blocking collectives: 40.8 us -> none  [on_device(): lax.all_gather(shares.astype(jnp.bfloat16), 'ctx', axis=0, tiled=True)]
    all_to_all x0 -> x6, starting transfers between devices: none -> 32.9 us  [the longest x1 10.4 us: on_device(): kv = lax.all_to_all(to_send, CTX, 0, 0).reshape(16 * BLK, 2 * HD)]
    dot_general x11 -> x2, matrix products: 26.2 us -> 1.99 us  [the longest x1 1.58 us: on_device(): jnp.einsum('ftd,ftc->dc', x_recv, gathered[:, 1], preferred_element_type=...]
  transfers between devices with their start and end apart: 3 -> 11, of which waited for: 3 -> 10; matrix products, arithmetic and copies ran while one was open for 2% -> 4% of each run, Pallas kernels for 0% -> 0%
where the time goes in v1:
time: 175 us; the launch traced here: 173 us
  waiting for transfers between devices  109 us (62%)
  starting transfers between devices  40.2 us (23%)
  Pallas kernels  7.76 us (4%)
  local copies, waits for them, and re-layouts  7.7 us (4%)
  other arithmetic  5.78 us (3%)
  matrix products  1.99 us (1%)
    ppermute x1, waiting for transfers between devices, on_device(): recv = lax.ppermute(halves((1 - g) * half), YAX, PARTNER)  19.6 us
    all_to_all x1, waiting for transfers between devices, on_device(): shares = lax.all_to_all(partial, Z, 0, 0)  14.8 us
    all_to_all x1, waiting for transfers between devices, on_device(): lax.all_to_all(jnp.broadcast_to(piece[None], (32,) + piece.shape), (DP, Y...  13.3 us
    ppermute x1, waiting for transfers between devices, on_device(): from_neighbour = lax.ppermute(theirs, YAX, NEIGHBOUR)  13 us
    all_to_all x1, waiting for transfers between devices, on_device(): lax.all_to_all(jnp.broadcast_to(both[None], (8,) + both.shape), FSDP, 0, 0)  12.6 us
    all_to_all x1, starting transfers between devices, on_device(): kv = lax.all_to_all(to_send, CTX, 0, 0).reshape(16 * BLK, 2 * HD)  10.4 us
    all_to_all x1, waiting for transfers between devices, on_device(): x_own = lax.all_to_all(x_out, FSDP, 0, 0)  8.64 us
    ppermute x1, waiting for transfers between devices, on_device(): x_recv = lax.ppermute(x_own, YAX, PARTNER)  8.28 us
  transfers between devices with their start and end apart: 11, of which 10 were waited for; matrix products, arithmetic and copies ran while one was open for 4% of the time, Pallas kernels for 0%

profile of v1, /device:TPU:32, one launch (start us, length us, event | category | flops | bytes accessed | tf_op | source)
XLA Modules:
  0.0 173.3 jit_solution(6828143167560605046)
XLA Ops:
  0.6 0.0 copy-start.4
  0.6 0.8 fusion.6
  1.5 0.0 copy-done.4
  1.6 1.1 pad_maximum_fusion
  2.7 0.0 copy-start.2
  2.7 0.0 copy-start.3
  2.7 10.4 %all-to-all-start = ((bf16[16,128,256]{2,1,0:T(8,128)(2,1)}), bf16[16,128,256]{2,1,0:T(8,128)(2,1)S(1)}, u32[]{:S(2)}, u32[]{:S(2)}) async-start(bf16[16,128,256]{2,1,0:T(8,128)(2,1)} %pad_maximum_fusion), calls=%async_computation | async-start | bytes 2097152 | tf_op jit(solution)/shard_map/all_to_all | solution.py:160
  13.1 0.0 copy-done.2
  13.1 0.0 copy-done.3
  13.1 0.1 dynamic-slice_bitcast_fusion
  13.3 3.2 %collective-permute-start = (bf16[256,896]{1,0:T(8,128)(2,1)S(1)}, bf16[256,896]{1,0:T(8,128)(2,1)S(1)}, u32[]{:S(2)}, u32[]{:S(2)}) collective-permute-start(bf16[256,896]{1,0:T(8,128)(2,1)S(1)} %pad_maximum_fusion.2), channel_id=1, source_target_pairs={{0,12},{12,0},{4,8},{8,4},{1,13},{13,1},{5,9},{9,5},{2,14},{14,2},... | collective-permute-start | bytes 1376264 | tf_op jit(solution)/shard_map/ppermute | solution.py:171
  16.5 0.1 stack.32.sc_ref
  16.6 0.0 copy-start
  16.6 19.6 %collective-permute-done.recv_ref = bf16[256,896]{1,0:T(8,128)(2,1)S(1)} collective-permute-done((bf16[256,896]{1,0:T(8,128)(2,1)S(1)}, bf16[256,896]{1,0:T(8,128)(2,1)S(1)}, u32[]{:S(2)}, u32[]{:S(2)}) %collective-permute-start) | collective-permute-done | bytes 458784 | tf_op jit(solution)/shard_map/ppermute | solution.py:171
  36.2 5.9 %all-to-all-done = bf16[16,128,256]{2,1,0:T(8,128)(2,1)S(1)} async-done(((bf16[16,128,256]{2,1,0:T(8,128)(2,1)}), bf16[16,128,256]{2,1,0:T(8,128)(2,1)S(1)}, u32[]{:S(2)}, u32[]{:S(2)}) %all-to-all-start) | async-done | bytes 1048608 | tf_op jit(solution)/shard_map/all_to_all | solution.py:160
  42.2 0.0 copy-done
  42.2 7.8 %shard_map.93 = (bf16[128,896]{1,0:T(8,128)(2,1)S(1)}, bf16[128,896]{1,0:T(8,128)(2,1)S(1)}, f32[4,2,128,256]{3,2,1,0:T(8,128)S(1)}, bf16[4,2,128,256]{3,2,1,0:T(8,128)(2,1)S(1)}) custom-call(s32[6]{0:T(128)S(1)} %stack.32.sc_ref, s32[16,128]{1,0:T(8,128)S(1)} %bitcast.61, bf16[256,896]{1,0:T(8,128)(2,1)S(1)} %pad_maximum_fusion.1.own_ref, ...), custom_call_target="tpu_custom_call" | custom-call | flops 5000000000 | bytes 8000000 | tf_op jit(solution)/shard_map/pallas_call | solution.py:121
  49.9 0.1 collective-permute-start.2
  50.0 13.0 %collective-permute-done.2 = bf16[4,2,128,256]{3,2,1,0:T(8,128)(2,1)S(1)} collective-permute-done((bf16[4,2,128,256]{3,2,1,0:T(8,128)(2,1)S(1)}, bf16[4,2,128,256]{3,2,1,0:T(8,128)(2,1)S(1)}, u32[]{:S(2)}, u32[]{:S(2)}) %collective-permute-start.2) | collective-permute-done | bytes 524320 | tf_op jit(solution)/shard_map/ppermute | solution.py:200
  63.0 1.0 add_convert_fusion
  64.0 0.0 copy-start.1
  64.0 6.2 %all-to-all-start.1 = ((bf16[4,2,128,256]{3,2,1,0:T(8,128)(2,1)}), bf16[4,2,128,256]{3,2,1,0:T(8,128)(2,1)S(1)}, u32[]{:S(2)}, u32[]{:S(2)}) async-start(bf16[4,2,128,256]{3,2,1,0:T(8,128)(2,1)} %add_convert_fusion), calls=%async_computation.1 | async-start | bytes 1048576 | tf_op jit(solution)/shard_map/all_to_all | solution.py:202
  70.2 0.0 copy-done.1
  70.2 1.3 copy.20
  71.4 14.8 %all-to-all-done.1 = bf16[4,2,128,256]{3,2,1,0:T(8,128)(2,1)S(1)} async-done(((bf16[4,2,128,256]{3,2,1,0:T(8,128)(2,1)}), bf16[4,2,128,256]{3,2,1,0:T(8,128)(2,1)S(1)}, u32[]{:S(2)}, u32[]{:S(2)}) %all-to-all-start.1) | async-done | bytes 524320 | tf_op jit(solution)/shard_map/all_to_all | solution.py:202
  86.2 3.6 %all-to-all-start.3 = ((bf16[8,128,448]{1,2,0:T(8,128)(2,1)}), bf16[8,128,448]{1,2,0:T(8,128)(2,1)S(1)}, u32[]{:S(2)}, u32[]{:S(2)}) async-start(bf16[8,128,448]{1,2,0:T(8,128)(2,1)} %bitcast.22), calls=%async_computation.3 | async-start | bytes 1835008 | tf_op jit(solution)/shard_map/all_to_all | solution.py:176
  89.8 0.1 reduce_sum.21
  89.9 0.6 collective-permute-start.3
  90.5 5.1 %collective-permute-done.3 = bf16[128,256]{1,0:T(8,128)(2,1)S(1)} collective-permute-done((bf16[128,256]{1,0:T(8,128)(2,1)S(1)}, bf16[128,256]{1,0:T(8,128)(2,1)S(1)}, u32[]{:S(2)}, u32[]{:S(2)}) %collective-permute-start.3) | collective-permute-done | bytes 65568 | tf_op jit(solution)/shard_map/ppermute | solution.py:206
  95.6 8.6 %all-to-all-done.3 = bf16[8,128,448]{1,2,0:T(8,128)(2,1)S(1)} async-done(((bf16[8,128,448]{1,2,0:T(8,128)(2,1)}), bf16[8,128,448]{1,2,0:T(8,128)(2,1)S(1)}, u32[]{:S(2)}, u32[]{:S(2)}) %all-to-all-start.3) | async-done | bytes 917536 | tf_op jit(solution)/shard_map/all_to_all | solution.py:176
  104.3 1.1 broadcast_in_dim.16
  105.4 3.6 %all-to-all-start.2 = ((bf16[8,2,128,256]{3,2,1,0:T(8,128)(2,1)}), bf16[8,2,128,256]{3,2,1,0:T(8,128)(2,1)S(1)}, u32[]{:S(2)}, u32[]{:S(2)}) async-start(bf16[8,2,128,256]{3,2,1,0:T(8,128)(2,1)} %broadcast_in_dim.16), calls=%async_computation.2 | async-start | bytes 2097152 | tf_op jit(solution)/shard_map/all_to_all | solution.py:212
  108.9 0.6 collective-permute-start.4
  109.5 2.7 %collective-permute-start.1 = (bf16[128,896]{1,0:T(8,128)(2,1)S(1)}, bf16[128,896]{1,0:T(8,128)(2,1)}, u32[]{:S(2)}, u32[]{:S(2)}) collective-permute-start(bf16[128,896]{1,0:T(8,128)(2,1)S(1)} %get-tuple-element.9), channel_id=1, source_target_pairs={{0,12},{12,0},{4,8},{8,4},{1,13},{13,1},{5,9},{9,5},{2,14},{14,2},... | collective-permute-start | bytes 688136 | tf_op jit(solution)/shard_map/ppermute | solution.py:193
  112.3 12.6 %all-to-all-done.2 = bf16[8,2,128,256]{3,2,1,0:T(8,128)(2,1)S(1)} async-done(((bf16[8,2,128,256]{3,2,1,0:T(8,128)(2,1)}), bf16[8,2,128,256]{3,2,1,0:T(8,128)(2,1)S(1)}, u32[]{:S(2)}, u32[]{:S(2)}) %all-to-all-start.2) | async-done | bytes 1048608 | tf_op jit(solution)/shard_map/all_to_all | solution.py:212
  124.8 0.4 convolution_bitcast_fusion.1
  125.2 8.3 %collective-permute-done.4 = bf16[8,128,448]{1,2,0:T(8,128)(2,1)} collective-permute-done((bf16[8,128,448]{1,2,0:T(8,128)(2,1)S(1)}, bf16[8,128,448]{1,2,0:T(8,128)(2,1)}, u32[]{:S(2)}, u32[]{:S(2)}) %collective-permute-start.4) | collective-permute-done | bytes 917536 | tf_op jit(solution)/shard_map/ppermute | solution.py:177
  133.5 1.6 fusion.2
  135.1 0.7 reshape.91
  135.8 4.2 %all-to-all-start.4 = ((bf16[16,28,256]{2,1,0:T(8,128)(2,1)}), bf16[16,28,256]{2,1,0:T(8,128)(2,1)S(1)}, u32[]{:S(2)}, u32[]{:S(2)}) async-start(bf16[16,28,256]{2,1,0:T(8,128)(2,1)} %reshape.91), calls=%async_computation.4 | async-start | bytes 524288 | tf_op jit(solution)/shard_map/all_to_all | solution.py:216
  140.1 0.0 collective-permute-done.1
  140.1 1.9 %maximum_select_fusion = bf16[1,128,1792]{2,1,0:T(8,128)(2,1)} fusion(bf16[1,128,896]{2,1,0:T(8,128)(2,1)} %bitcast.15, bf16[1,128,896]{2,1,0:T(8,128)(2,1)S(1)} %bitcast.60, pred[]{:T(512)S(6)} %eq.11), kind=kLoop, calls=%fused_computation.12 | loop fusion | flops 2064384 | bytes 917505 | tf_op jit(solution)/shard_map/jit(_where)/select_n | solution.py:194
  142.0 7.9 %all-to-all-done.4 = bf16[16,28,256]{2,1,0:T(8,128)(2,1)S(1)} async-done(((bf16[16,28,256]{2,1,0:T(8,128)(2,1)}), bf16[16,28,256]{2,1,0:T(8,128)(2,1)S(1)}, u32[]{:S(2)}, u32[]{:S(2)}) %all-to-all-start.4) | async-done | bytes 229408 | tf_op jit(solution)/shard_map/all_to_all | solution.py:216
  150.0 0.9 broadcast_in_dim.17
  150.8 4.9 %all-to-all-start.5 = ((bf16[32,28,256]{2,1,0:T(8,128)(2,1)}), bf16[32,28,256]{2,1,0:T(8,128)(2,1)S(1)}, u32[]{:S(2)}, u32[]{:S(2)}) async-start(bf16[32,28,256]{2,1,0:T(8,128)(2,1)} %broadcast_in_dim.17), calls=%async_computation.5 | async-start | bytes 1048576 | tf_op jit(solution)/shard_map/all_to_all | solution.py:219
  155.8 0.6 maximum_bitcast_fusion
  156.5 0.6 maximum_bitcast_fusion.1
  157.1 13.3 %all-to-all-done.5 = bf16[32,28,256]{2,1,0:T(8,128)(2,1)S(1)} async-done(((bf16[32,28,256]{2,1,0:T(8,128)(2,1)}), bf16[32,28,256]{2,1,0:T(8,128)(2,1)S(1)}, u32[]{:S(2)}, u32[]{:S(2)}) %all-to-all-start.5) | async-done | bytes 458784 | tf_op jit(solution)/shard_map/all_to_all | solution.py:219
  170.4 0.3 copy_convert_fusion
  170.7 0.5 reshape.93
  171.1 0.5 copy.23
  171.6 1.7 reshape.92
  (15 shorter events, 0.3 us)
Async XLA Ops:
  0.6 0.8 copy-start.4
  2.7 10.5 %copy-start.2 = (bf16[1,128,1792]{2,1,0:T(8,128)(2,1)S(1)}, bf16[1,128,1792]{2,1,0:T(8,128)(2,1)}, u32[]{:S(2)}) copy-start(bf16[1,128,1792]{2,1,0:T(8,128)(2,1)} %param.9) | copy-start | bytes 1376260
  2.7 10.5 %copy-start.3 = (bf16[1,128,1792]{2,1,0:T(8,128)(2,1)S(1)}, bf16[1,128,1792]{2,1,0:T(8,128)(2,1)}, u32[]{:S(2)}) copy-start(bf16[1,128,1792]{2,1,0:T(8,128)(2,1)} %param.6) | copy-start | bytes 1376260
  2.7 39.5 %all-to-all-start = ((bf16[16,128,256]{2,1,0:T(8,128)(2,1)}), bf16[16,128,256]{2,1,0:T(8,128)(2,1)S(1)}, u32[]{:S(2)}, u32[]{:S(2)}) async-start(bf16[16,128,256]{2,1,0:T(8,128)(2,1)} %pad_maximum_fusion), calls=%async_computation | async-start | bytes 2097152 | tf_op jit(solution)/shard_map/all_to_all | solution.py:160
  13.3 23.0 %collective-permute-start = (bf16[256,896]{1,0:T(8,128)(2,1)S(1)}, bf16[256,896]{1,0:T(8,128)(2,1)S(1)}, u32[]{:S(2)}, u32[]{:S(2)}) collective-permute-start(bf16[256,896]{1,0:T(8,128)(2,1)S(1)} %pad_maximum_fusion.2), channel_id=1, source_target_pairs={{0,12},{12,0},{4,8},{8,4},{1,13},{13,1},{5,9},{9,5},{2,14},{14,2},... | collective-permute-start | bytes 1376264 | tf_op jit(solution)/shard_map/ppermute | solution.py:171
  16.6 25.6 %copy-start = (s32[1,2048]{1,0:T(1,128)S(1)}, s32[1,2048]{1,0:T(1,128)}, u32[]{:S(2)}) copy-start(s32[1,2048]{1,0:T(1,128)} %param.11) | copy-start | bytes 24580
  49.9 13.1 %collective-permute-start.2 = (bf16[4,2,128,256]{3,2,1,0:T(8,128)(2,1)S(1)}, bf16[4,2,128,256]{3,2,1,0:T(8,128)(2,1)S(1)}, u32[]{:S(2)}, u32[]{:S(2)}) collective-permute-start(bf16[4,2,128,256]{3,2,1,0:T(8,128)(2,1)S(1)} %get-tuple-element.11), channel_id=1, source_target_pairs={{0,4},{4,0},{8,12},{12,8},{1,5},{5,1},{9,13},{13,9},{2,6},{6,2},{1... | collective-permute-start | bytes 1572872 | tf_op jit(solution)/shard_map/ppermute | solution.py:200
  64.0 6.2 %copy-start.1 = (bf16[1,128,3584]{2,1,0:T(8,128)(2,1)S(1)}, bf16[1,128,3584]{2,1,0:T(8,128)(2,1)}, u32[]{:S(2)}) copy-start(bf16[1,128,3584]{2,1,0:T(8,128)(2,1)} %param.10) | copy-start | bytes 2752516
  64.0 22.2 %all-to-all-start.1 = ((bf16[4,2,128,256]{3,2,1,0:T(8,128)(2,1)}), bf16[4,2,128,256]{3,2,1,0:T(8,128)(2,1)S(1)}, u32[]{:S(2)}, u32[]{:S(2)}) async-start(bf16[4,2,128,256]{3,2,1,0:T(8,128)(2,1)} %add_convert_fusion), calls=%async_computation.1 | async-start | bytes 1048576 | tf_op jit(solution)/shard_map/all_to_all | solution.py:202
  86.2 18.0 %all-to-all-start.3 = ((bf16[8,128,448]{1,2,0:T(8,128)(2,1)}), bf16[8,128,448]{1,2,0:T(8,128)(2,1)S(1)}, u32[]{:S(2)}, u32[]{:S(2)}) async-start(bf16[8,128,448]{1,2,0:T(8,128)(2,1)} %bitcast.22), calls=%async_computation.3 | async-start | bytes 1835008 | tf_op jit(solution)/shard_map/all_to_all | solution.py:176
  89.9 5.7 %collective-permute-start.3 = (bf16[128,256]{1,0:T(8,128)(2,1)S(1)}, bf16[128,256]{1,0:T(8,128)(2,1)S(1)}, u32[]{:S(2)}, u32[]{:S(2)}) collective-permute-start(bf16[128,256]{1,0:T(8,128)(2,1)S(1)} %fusion.9), channel_id=1, source_target_pairs={{0,12},{12,0},{4,8},{8,4},{1,13},{13,1},{5,9},{9,5},{2,14},{14,2},... | collective-permute-start | bytes 196616 | tf_op jit(solution)/shard_map/ppermute | solution.py:206
  105.4 19.4 %all-to-all-start.2 = ((bf16[8,2,128,256]{3,2,1,0:T(8,128)(2,1)}), bf16[8,2,128,256]{3,2,1,0:T(8,128)(2,1)S(1)}, u32[]{:S(2)}, u32[]{:S(2)}) async-start(bf16[8,2,128,256]{3,2,1,0:T(8,128)(2,1)} %broadcast_in_dim.16), calls=%async_computation.2 | async-start | bytes 2097152 | tf_op jit(solution)/shard_map/all_to_all | solution.py:212
  108.9 24.6 %collective-permute-start.4 = (bf16[8,128,448]{1,2,0:T(8,128)(2,1)S(1)}, bf16[8,128,448]{1,2,0:T(8,128)(2,1)}, u32[]{:S(2)}, u32[]{:S(2)}) collective-permute-start(bf16[8,128,448]{1,2,0:T(8,128)(2,1)S(1)} %all-to-all-done.3), channel_id=1, source_target_pairs={{0,12},{12,0},{4,8},{8,4},{1,13},{13,1},{5,9},{9,5},{2,14},{14,2},... | collective-permute-start | bytes 2752520 | tf_op jit(solution)/shard_map/ppermute | solution.py:177
  109.5 30.6 %collective-permute-start.1 = (bf16[128,896]{1,0:T(8,128)(2,1)S(1)}, bf16[128,896]{1,0:T(8,128)(2,1)}, u32[]{:S(2)}, u32[]{:S(2)}) collective-permute-start(bf16[128,896]{1,0:T(8,128)(2,1)S(1)} %get-tuple-element.9), channel_id=1, source_target_pairs={{0,12},{12,0},{4,8},{8,4},{1,13},{13,1},{5,9},{9,5},{2,14},{14,2},... | collective-permute-start | bytes 688136 | tf_op jit(solution)/shard_map/ppermute | solution.py:193
  135.8 14.1 %all-to-all-start.4 = ((bf16[16,28,256]{2,1,0:T(8,128)(2,1)}), bf16[16,28,256]{2,1,0:T(8,128)(2,1)S(1)}, u32[]{:S(2)}, u32[]{:S(2)}) async-start(bf16[16,28,256]{2,1,0:T(8,128)(2,1)} %reshape.91), calls=%async_computation.4 | async-start | bytes 524288 | tf_op jit(solution)/shard_map/all_to_all | solution.py:216
  150.8 19.6 %all-to-all-start.5 = ((bf16[32,28,256]{2,1,0:T(8,128)(2,1)}), bf16[32,28,256]{2,1,0:T(8,128)(2,1)S(1)}, u32[]{:S(2)}, u32[]{:S(2)}) async-start(bf16[32,28,256]{2,1,0:T(8,128)(2,1)} %broadcast_in_dim.17), calls=%async_computation.5 | async-start | bytes 1048576 | tf_op jit(solution)/shard_map/all_to_all | solution.py:219

commit v2 on v1

--- a/solution.py
+++ b/solution.py
@@ -19,14 +19,20 @@
 CTX = (YH, YL, Z)
 PARTNER = [(0, 3), (3, 0), (1, 2), (2, 1)]
 NEIGHBOUR = [(0, 1), (1, 0), (2, 3), (3, 2)]
+OPPOSITE = [(0, 2), (2, 0), (1, 3)]
 
 
 def attention_kernel(
-    sc_ref, seg_ref, own_ref, recv_ref, kv_ref,
+    sc_ref, seg_ref, own_ref, recv_ref, kv0_ref, kv1_ref, kv2_ref, kv3_ref, ahead_ref,
     dq_own_ref, dq_recv_ref, mine_ref, theirs_ref,
-    s_ref, dp_ref, kt_ref, acc_ref, dqt_ref,
+    s_ref, dp_ref, kt_ref, acc_ref, dqt_ref, kv_ref,
 ):
+    del ahead_ref
     length = kv_ref.shape[0]
+    for i, part_ref in enumerate((kv0_ref, kv1_ref, kv2_ref, kv3_ref)):
+        for d in range(4):
+            at = pl.multiple_of(sc_ref[6 + i] * (length // 4) + sc_ref[10 + d] * BLK, BLK)
+            kv_ref[pl.ds(at, BLK), :] = part_ref[d]
     tiles = length // KT
     rows = GS * BLK
     nt = (((1,), (1,)), ((), ()))
@@ -114,8 +120,35 @@
             theirs_ref[z, j] = acc_ref[pl.ds(at, BLK), :].astype(bf16)
 
 
-def attention(scalars, seg, own, recv, kv):
-    length = kv.shape[0]
+def split_kernel(sc_ref, a_ref, b_ref, c_ref, d_ref, own_ref, other_ref):
+    def write(first, second):
+        for i, ref in enumerate((a_ref, b_ref, c_ref, d_ref)):
+            for out, g in ((first, 0), (second, 1)):
+                out[i, :, 0:HD] = ref[:, g * HD:(g + 1) * HD]
+                out[i, :, HD:2 * HD] = ref[:, (2 + g) * HD:(3 + g) * HD]
+
+    @pl.when(sc_ref[0] == 0)
+    def _():
+        write(own_ref, other_ref)
+
+    @pl.when(sc_ref[0] != 0)
+    def _():
+        write(other_ref, own_ref)
+
+
+def split_groups(group, blocks):
+    vmem = pl.BlockSpec(memory_space=pltpu.VMEM)
+    shape = jax.ShapeDtypeStruct((4, BLK, 2 * HD), jnp.bfloat16)
+    return pl.pallas_call(
+        split_kernel,
+        out_shape=(shape, shape),
+        in_specs=[pl.BlockSpec(memory_space=pltpu.SMEM)] + [vmem] * 4,
+        out_specs=(vmem, vmem),
+    )(group, *blocks)
+
+
+def attention(scalars, seg, own, recv, kvs, ahead):
+    length = 4 * kvs[0].shape[0] * kvs[0].shape[1]
     rows = GS * BLK
     vmem = pl.BlockSpec(memory_space=pltpu.VMEM)
     return pl.pallas_call(
@@ -126,7 +159,7 @@
             jax.ShapeDtypeStruct((4, 2, BLK, 2 * HD), jnp.float32),
             jax.ShapeDtypeStruct((4, 2, BLK, 2 * HD), jnp.bfloat16),
         ),
-        in_specs=[pl.BlockSpec(memory_space=pltpu.SMEM), vmem, vmem, vmem, vmem],
+        in_specs=[pl.BlockSpec(memory_space=pltpu.SMEM)] + [vmem] * 7 + [pl.BlockSpec(memory_space=pl.ANY)],
         out_specs=(vmem, vmem, vmem, vmem),
         scratch_shapes=[
             pltpu.VMEM((length, rows), jnp.float32),
@@ -134,12 +167,13 @@
             pltpu.VMEM((length // KT, HD, KT), jnp.bfloat16),
             pltpu.VMEM((length, 2 * HD), jnp.float32),
             pltpu.VMEM((HD, rows), jnp.float32),
+            pltpu.VMEM((length, 2 * HD), jnp.bfloat16),
         ],
         compiler_params=pltpu.CompilerParams(vmem_limit_bytes=48 * 1024 * 1024),
         cost_estimate=pl.CostEstimate(
             flops=5_000_000_000, bytes_accessed=8_000_000, transcendentals=4_000_000
         ),
-    )(scalars, seg, own, recv, kv)
+    )(scalars, seg, own, recv, *kvs, ahead)
 
 
 def on_device(queries, key_states, value_states, out_grad, layer_input, segment_ids):
@@ -149,15 +183,15 @@
     z = lax.axis_index(Z)
     g = lax.axis_index(YH)
     half = GS * HD
-    k, v = key_states[0], value_states[0]
-    kv_groups = [
-        jnp.concatenate([k[:, i * HD:(i + 1) * HD], v[:, i * HD:(i + 1) * HD]], axis=1)
-        for i in range(GROUPS)
-    ]
-    to_send = jnp.concatenate(
-        [jnp.broadcast_to(x[None], (8, BLK, 2 * HD)) for x in kv_groups], axis=0
-    )
-    kv = lax.all_to_all(to_send, CTX, 0, 0).reshape(16 * BLK, 2 * HD)
+    raw = jnp.concatenate([key_states[0], value_states[0]], axis=1)
+    around = [raw] + [lax.ppermute(raw, Z, [(i, (i + d) % 4) for i in range(4)]) for d in (1, 2, 3)]
+    kv_own, kv_other = split_groups(g.astype(jnp.int32)[None], around)
+    kvs = (
+        kv_own,
+        lax.ppermute(kv_other, YAX, OPPOSITE),
+        lax.ppermute(kv_other, YAX, PARTNER),
+        lax.ppermute(kv_own, YAX, [(0, 1), (1, 0), (2, 3)]),
+    )
 
     def halves(at):
         return jnp.concatenate(
@@ -175,6 +209,19 @@
     x_out = layer_input[0].reshape(BLK, 8, features).transpose(1, 0, 2)
     x_own = lax.all_to_all(x_out, FSDP, 0, 0)
     x_recv = lax.ppermute(x_own, YAX, PARTNER)
+    fx = lax.axis_index(FX)
+    fc = lax.axis_index(FC)
+
+    def arranged(core):
+        rows = [
+            lax.dynamic_index_in_dim(x, ((fx - d) % 4) * 2 + core, 0, keepdims=False)
+            for d in range(4)
+            for x in (x_own, x_recv)
+        ]
+        return jnp.stack(rows)
+
+    x_near = arranged(fc)
+    x_far = arranged(1 - fc)
 
     middle = ((y == 1) | (y == 2)).astype(jnp.int32)
     scalars = jnp.stack(
@@ -185,10 +232,18 @@
             3 - middle,
             1 - middle,
             2 + middle,
+            y,
+            (y + 2) % 4,
+            3 - y,
+            y + 1 - 2 * (y % 2),
+            z,
+            (z + 3) % 4,
+            (z + 2) % 4,
+            (z + 1) % 4,
         ]
     ).astype(jnp.int32)
     dq_own, dq_recv, mine, theirs = attention(
-        scalars, segment_ids.reshape(16, 128), own, recv, kv
+        scalars, segment_ids.reshape(16, 128), own, recv, kvs, x_own
     )
     dq_other = lax.ppermute(dq_recv, YAX, PARTNER)
     query_grad = jnp.where(
@@ -199,8 +254,12 @@
 
     from_neighbour = lax.ppermute(theirs, YAX, NEIGHBOUR)
     partial = (mine + from_neighbour.astype(f32)).astype(bf16)
-    shares = lax.all_to_all(partial, Z, 0, 0)
-    kv_grad = jnp.sum(shares.astype(f32), axis=0).astype(bf16)
+    total = lax.dynamic_index_in_dim(partial, z, 0, keepdims=False).astype(f32)
+    for d in (1, 2, 3):
+        piece = lax.dynamic_index_in_dim(partial, (z + d) % 4, 0, keepdims=False)
+        piece = lax.ppermute(piece, Z, [(i, (i + d) % 4) for i in range(4)])
+        total = total + piece.astype(f32)
+    kv_grad = total.astype(bf16)
     grad_own = lax.dynamic_index_in_dim(kv_grad, g, 0, keepdims=False)
     grad_partner = lax.dynamic_index_in_dim(kv_grad, 1 - g, 0, keepdims=False)
     grad_other = lax.ppermute(grad_partner, YAX, PARTNER)
@@ -209,9 +268,12 @@
     value_grad = jnp.concatenate([x[:, HD:] for x in grads], axis=1)
 
     both = jnp.stack([grad_own, grad_partner])
-    gathered = lax.all_to_all(jnp.broadcast_to(both[None], (8,) + both.shape), FSDP, 0, 0)
-    part = jnp.einsum("ftd,ftc->dc", x_own, gathered[:, 0], preferred_element_type=f32)
-    part = part + jnp.einsum("ftd,ftc->dc", x_recv, gathered[:, 1], preferred_element_type=f32)
+    near = jnp.concatenate(
+        [both] + [lax.ppermute(both, FX, [(i, (i + d) % 4) for i in range(4)]) for d in (1, 2, 3)]
+    )
+    far = lax.ppermute(near, FC, [(0, 1), (1, 0)])
+    part = jnp.einsum("etd,etc->dc", x_near, near, preferred_element_type=f32)
+    part = part + jnp.einsum("etd,etc->dc", x_far, far, preferred_element_type=f32)
     pieces = part.astype(bf16).reshape(16, features // 16, 2 * HD)
     pieces = lax.all_to_all(pieces, (DP, YL, Z), 0, 0)
     tokens = BLK * 256

time: 175 us -> 160 us (0.914)
  waiting for transfers between devices: 109 us -> 64.1 us
  starting transfers between devices: 40.2 us -> 64.4 us
  local copies, waits for them, and re-layouts: 7.7 us -> 20.7 us
  other arithmetic: 5.78 us -> 2.78 us
  Pallas kernels: 7.76 us -> 5.54 us
    ppermute x0 -> x13, starting transfers between devices: none -> 35.1 us  [the longest x3 10.5 us: on_device(): lax.ppermute(raw, Z, [(i, (i + d) % 4) for i in range(4)])]
    all_to_all x3 -> x0, waiting for transfers between devices: 33.3 us -> none  [the longest x1 14.8 us: on_device(): shares = lax.all_to_all(partial, Z, 0, 0)]
    ppermute x0 -> x13, waiting for transfers between devices: none -> 25.5 us  [the longest x3 8.44 us: on_device(): piece = lax.ppermute(piece, Z, [(i, (i + d) % 4) for i in range(4)])]
    all_to_all x3 -> x0, starting transfers between devices: 20.2 us -> none  [the longest x1 10.4 us: on_device(): kv = lax.all_to_all(to_send, CTX, 0, 0).reshape(16 * BLK, 2 * HD)]
    ppermute x1, waiting for transfers between devices: 19.6 us -> 0.01 us  [on_device(): recv = lax.ppermute(halves((1 - g) * half), YAX, PARTNER)]
    unnamed x11 -> x48, local copies, waits for them, and re-layouts: 1.3 us -> 14.8 us
    all_to_all x1, waiting for transfers between devices: 8.64 us -> 0.01 us  [on_device(): x_own = lax.all_to_all(x_out, FSDP, 0, 0)]
    ppermute x1, waiting for transfers between devices: 8.28 us -> 1.77 us  [on_device(): x_recv = lax.ppermute(x_own, YAX, PARTNER)]
  transfers between devices with their start and end apart: 11 -> 21, of which waited for: 10 -> 13; matrix products, arithmetic and copies ran while one was open for 4% -> 7% of each run, Pallas kernels for 0% -> 1%
where the time goes in v2:
time: 160 us; the launch traced here: 159 us
  starting transfers between devices  64.4 us (40%)
  waiting for transfers between devices  64.1 us (40%)
  local copies, waits for them, and re-layouts  20.7 us (13%)
  Pallas kernels  5.54 us (3%)
  other arithmetic  2.78 us (2%)
    unnamed x48, local copies, waits for them, and re-layouts  14.8 us
    all_to_all x1, waiting for transfers between devices, on_device(): lax.all_to_all(jnp.broadcast_to(piece[None], (32,) + piece.shape), (DP, Y...  14.7 us
    ppermute x1, waiting for transfers between devices, on_device(): from_neighbour = lax.ppermute(theirs, YAX, NEIGHBOUR)  12.4 us
    ppermute x3, starting transfers between devices, on_device(): lax.ppermute(raw, Z, [(i, (i + d) % 4) for i in range(4)])  10.5 us
    all_to_all x1, waiting for transfers between devices, on_device(): pieces = lax.all_to_all(pieces, (DP, YL, Z), 0, 0)  9.73 us
    ppermute x3, starting transfers between devices, on_device(): piece = lax.ppermute(piece, Z, [(i, (i + d) % 4) for i in range(4)])  9.59 us
    ppermute x3, waiting for transfers between devices, on_device(): piece = lax.ppermute(piece, Z, [(i, (i + d) % 4) for i in range(4)])  8.44 us
    all_to_all x1, starting transfers between devices, on_device(): pieces = lax.all_to_all(pieces, (DP, YL, Z), 0, 0)  7.84 us
  transfers between devices with their start and end apart: 21, of which 13 were waited for; matrix products, arithmetic and copies ran while one was open for 7% of the time, Pallas kernels for 1%

profile of v2, /device:TPU:32, one launch (start us, length us, event | category | flops | bytes accessed | tf_op | source)
XLA Modules:
  0.0 159.4 jit_solution(9811007835724219708)
XLA Ops:
  0.6 2.2 %copy.25 = bf16[1,128,3584]{1,2,0:T(8,128)(2,1)} copy(bf16[1,128,3584]{2,1,0:T(8,128)(2,1)} %param.10) | data formatting | bytes 1835008 | tf_op args[4]
  2.8 4.4 %all-to-all-start = ((bf16[8,128,448]{1,2,0:T(8,128)(2,1)}), bf16[8,128,448]{1,2,0:T(8,128)(2,1)}, u32[]{:S(2)}, u32[]{:S(2)}) async-start(bf16[8,128,448]{1,2,0:T(8,128)(2,1)} %bitcast.23), calls=%async_computation | async-start | bytes 1835008 | tf_op jit(solution)/shard_map/all_to_all | solution.py:210
  7.3 0.1 dynamic-slice_bitcast_fusion
  7.5 3.1 %collective-permute-start = (bf16[256,896]{1,0:T(8,128)(2,1)S(1)}, bf16[256,896]{1,0:T(8,128)(2,1)S(1)}, u32[]{:S(2)}, u32[]{:S(2)}) collective-permute-start(bf16[256,896]{1,0:T(8,128)(2,1)S(1)} %pad_maximum_fusion.1), channel_id=1, source_target_pairs={{0,12},{12,0},{4,8},{8,4},{1,13},{13,1},{5,9},{9,5},{2,14},{14,2},... | collective-permute-start | bytes 1376264 | tf_op jit(solution)/shard_map/ppermute | solution.py:205
  10.6 3.3 %collective-permute-start.1 = (bf16[128,512]{1,0:T(8,128)(2,1)S(1)}, bf16[128,512]{1,0:T(8,128)(2,1)S(1)}, u32[]{:S(2)}, u32[]{:S(2)}) collective-permute-start(bf16[128,512]{1,0:T(8,128)(2,1)S(1)} %pad_maximum_fusion.2.a_ref), channel_id=1, source_target_pairs={{0,1},{1,2},{2,3},{3,0},{4,5},{5,6},{6,7},{7,4},{8,9},{9,10},{10,1... | collective-permute-start | bytes 393224 | tf_op jit(solution)/shard_map/ppermute | solution.py:187
  13.9 4.5 %collective-permute-start.2 = (bf16[128,512]{1,0:T(8,128)(2,1)S(1)}, bf16[128,512]{1,0:T(8,128)(2,1)S(1)}, u32[]{:S(2)}, u32[]{:S(2)}) collective-permute-start(bf16[128,512]{1,0:T(8,128)(2,1)S(1)} %pad_maximum_fusion.2.a_ref), channel_id=1, source_target_pairs={{0,2},{1,3},{2,0},{3,1},{4,6},{5,7},{6,4},{7,5},{8,10},{9,11},{10,... | collective-permute-start | bytes 393224 | tf_op jit(solution)/shard_map/ppermute | solution.py:187
  18.4 2.7 %collective-permute-start.3 = (bf16[128,512]{1,0:T(8,128)(2,1)S(1)}, bf16[128,512]{1,0:T(8,128)(2,1)S(1)}, u32[]{:S(2)}, u32[]{:S(2)}) collective-permute-start(bf16[128,512]{1,0:T(8,128)(2,1)S(1)} %pad_maximum_fusion.2.a_ref), channel_id=1, source_target_pairs={{0,3},{1,0},{2,1},{3,2},{4,7},{5,4},{6,5},{7,6},{8,11},{9,8},{10,9... | collective-permute-start | bytes 393224 | tf_op jit(solution)/shard_map/ppermute | solution.py:187
  21.1 2.3 %collective-permute-done.1.b_ref = bf16[128,512]{1,0:T(8,128)(2,1)S(1)} collective-permute-done((bf16[128,512]{1,0:T(8,128)(2,1)S(1)}, bf16[128,512]{1,0:T(8,128)(2,1)S(1)}, u32[]{:S(2)}, u32[]{:S(2)}) %collective-permute-start.1) | collective-permute-done | bytes 131104 | tf_op jit(solution)/shard_map/ppermute | solution.py:187
  23.5 2.6 %collective-permute-done.2.c_ref = bf16[128,512]{1,0:T(8,128)(2,1)S(1)} collective-permute-done((bf16[128,512]{1,0:T(8,128)(2,1)S(1)}, bf16[128,512]{1,0:T(8,128)(2,1)S(1)}, u32[]{:S(2)}, u32[]{:S(2)}) %collective-permute-start.2) | collective-permute-done | bytes 131104 | tf_op jit(solution)/shard_map/ppermute | solution.py:187
  26.1 2.7 %collective-permute-done.3.d_ref = bf16[128,512]{1,0:T(8,128)(2,1)S(1)} collective-permute-done((bf16[128,512]{1,0:T(8,128)(2,1)S(1)}, bf16[128,512]{1,0:T(8,128)(2,1)S(1)}, u32[]{:S(2)}, u32[]{:S(2)}) %collective-permute-start.3) | collective-permute-done | bytes 131104 | tf_op jit(solution)/shard_map/ppermute | solution.py:187
  28.8 0.7 copy-done.15
  29.4 2.0 %shard_map.93 = (bf16[4,128,256]{2,1,0:T(8,128)(2,1)}, bf16[4,128,256]{2,1,0:T(8,128)(2,1)}) custom-call(s32[1]{0:T(128)} %bitcast.19.sc_ref, bf16[128,512]{1,0:T(8,128)(2,1)} %copy-done.10, bf16[128,512]{1,0:T(8,128)(2,1)} %copy-done.13, bf16[128,512]{1,0:T(8,128)(2,1)} %copy-done.14, bf16[128,512]{1,0:T(8,128)(2,1)} %copy-done.15), custom_call_target="tpu_custom_call" | custom-call | tf_op jit(solution)/shard_map/pallas_call | solution.py:142
  31.4 3.1 %collective-permute-start.4 = (bf16[4,128,256]{2,1,0:T(8,128)(2,1)}, bf16[4,128,256]{2,1,0:T(8,128)(2,1)S(1)}, u32[]{:S(2)}, u32[]{:S(2)}) collective-permute-start(bf16[4,128,256]{2,1,0:T(8,128)(2,1)} %get-tuple-element.11), channel_id=1, source_target_pairs={{0,8},{8,0},{4,12},{1,9},{9,1},{5,13},{2,10},{10,2},{6,14},{3,11},... | collective-permute-start | bytes 786440 | tf_op jit(solution)/shard_map/ppermute | solution.py:191
  34.6 4.2 %collective-permute-start.6 = (bf16[4,128,256]{2,1,0:T(8,128)(2,1)}, bf16[4,128,256]{2,1,0:T(8,128)(2,1)S(1)}, u32[]{:S(2)}, u32[]{:S(2)}) collective-permute-start(bf16[4,128,256]{2,1,0:T(8,128)(2,1)} %get-tuple-element.10.kv0_ref), channel_id=1, source_target_pairs={{0,4},{4,0},{8,12},{1,5},{5,1},{9,13},{2,6},{6,2},{10,14},{3,7},{7... | collective-permute-start | bytes 786440 | tf_op jit(solution)/shard_map/ppermute | solution.py:193
  39.0 1.5 copy.26.ahead_ref
  40.5 3.2 %collective-permute-done.4.kv1_ref = bf16[4,128,256]{2,1,0:T(8,128)(2,1)S(1)} collective-permute-done((bf16[4,128,256]{2,1,0:T(8,128)(2,1)}, bf16[4,128,256]{2,1,0:T(8,128)(2,1)S(1)}, u32[]{:S(2)}, u32[]{:S(2)}) %collective-permute-start.4) | collective-permute-done | bytes 262176 | tf_op jit(solution)/shard_map/ppermute | solution.py:191
  43.8 0.7 copy-done.3
  44.5 3.4 %collective-permute-done.5.kv2_ref = bf16[4,128,256]{2,1,0:T(8,128)(2,1)S(1)} collective-permute-done((bf16[4,128,256]{2,1,0:T(8,128)(2,1)}, bf16[4,128,256]{2,1,0:T(8,128)(2,1)S(1)}, u32[]{:S(2)}, u32[]{:S(2)}) %collective-permute-start.5) | collective-permute-done | bytes 262176 | tf_op jit(solution)/shard_map/ppermute | solution.py:192
  47.8 0.7 copy-done.5
  48.6 0.7 copy-done.7
  49.3 0.8 copy-done
  50.0 1.0 copy-done.1
  51.1 0.9 copy-done.2
  52.0 0.9 copy-done.4
  53.0 0.9 copy-done.6
  53.9 0.9 copy-done.8
  54.9 3.6 %shard_map.94 = (bf16[128,896]{1,0:T(8,128)(2,1)S(1)}, bf16[128,896]{1,0:T(8,128)(2,1)S(1)}, f32[4,2,128,256]{3,2,1,0:T(8,128)S(1)}, bf16[4,2,128,256]{3,2,1,0:T(8,128)(2,1)S(1)}) custom-call(s32[14]{0:T(128)S(1)} %stack.86.sc_ref, s32[16,128]{1,0:T(8,128)S(1)} %bitcast.64, bf16[256,896]{1,0:T(8,128)(2,1)S(1)} %pad_maximum_fusion.own_ref, ...), custom_call_target="tpu_custom_call" | custom-call | flops 5000000000 | bytes 8000000 | tf_op jit(solution)/shard_map/pallas_call | solution.py:154
  58.4 5.9 %collective-permute-start.8 = (bf16[4,2,128,256]{3,2,1,0:T(8,128)(2,1)S(1)}, bf16[4,2,128,256]{3,2,1,0:T(8,128)(2,1)S(1)}, u32[]{:S(2)}, u32[]{:S(2)}) collective-permute-start(bf16[4,2,128,256]{3,2,1,0:T(8,128)(2,1)S(1)} %get-tuple-element.15), channel_id=1, source_target_pairs={{0,4},{4,0},{8,12},{12,8},{1,5},{5,1},{9,13},{13,9},{2,6},{6,2},{1... | collective-permute-start | bytes 1572872 | tf_op jit(solution)/shard_map/ppermute | solution.py:255
  64.3 12.4 %collective-permute-done.8 = bf16[4,2,128,256]{3,2,1,0:T(8,128)(2,1)S(1)} collective-permute-done((bf16[4,2,128,256]{3,2,1,0:T(8,128)(2,1)S(1)}, bf16[4,2,128,256]{3,2,1,0:T(8,128)(2,1)S(1)}, u32[]{:S(2)}, u32[]{:S(2)}) %collective-permute-start.8) | collective-permute-done | bytes 524320 | tf_op jit(solution)/shard_map/ppermute | solution.py:255
  76.7 0.1 add_convert_fusion
  76.9 5.8 %collective-permute-start.11 = (bf16[2,128,256]{2,1,0:T(8,128)(2,1)S(1)}, bf16[2,128,256]{2,1,0:T(8,128)(2,1)S(1)}, u32[]{:S(2)}, u32[]{:S(2)}) collective-permute-start(bf16[2,128,256]{2,1,0:T(8,128)(2,1)S(1)} %get-tuple-element.37), channel_id=1, source_target_pairs={{0,3},{1,0},{2,1},{3,2},{4,7},{5,4},{6,5},{7,6},{8,11},{9,8},{10,9... | collective-permute-start | bytes 393224 | tf_op jit(solution)/shard_map/ppermute | solution.py:260
  82.7 1.0 collective-permute-start.10
  83.7 2.8 %collective-permute-start.9 = (bf16[2,128,256]{2,1,0:T(8,128)(2,1)S(1)}, bf16[2,128,256]{2,1,0:T(8,128)(2,1)S(1)}, u32[]{:S(2)}, u32[]{:S(2)}) collective-permute-start(bf16[2,128,256]{2,1,0:T(8,128)(2,1)S(1)} %get-tuple-element.36), channel_id=1, source_target_pairs={{0,1},{1,2},{2,3},{3,0},{4,5},{5,6},{6,7},{7,4},{8,9},{9,10},{10,1... | collective-permute-start | bytes 393224 | tf_op jit(solution)/shard_map/ppermute | solution.py:260
  86.5 1.2 collective-permute-start.13
  87.7 1.7 %collective-permute-done.11 = bf16[2,128,256]{2,1,0:T(8,128)(2,1)S(1)} collective-permute-done((bf16[2,128,256]{2,1,0:T(8,128)(2,1)S(1)}, bf16[2,128,256]{2,1,0:T(8,128)(2,1)S(1)}, u32[]{:S(2)}, u32[]{:S(2)}) %collective-permute-start.11) | collective-permute-done | bytes 131104 | tf_op jit(solution)/shard_map/ppermute | solution.py:260
  89.4 6.7 %collective-permute-done.10 = bf16[2,128,256]{2,1,0:T(8,128)(2,1)S(1)} collective-permute-done((bf16[2,128,256]{2,1,0:T(8,128)(2,1)S(1)}, bf16[2,128,256]{2,1,0:T(8,128)(2,1)S(1)}, u32[]{:S(2)}, u32[]{:S(2)}) %collective-permute-start.10) | collective-permute-done | bytes 131104 | tf_op jit(solution)/shard_map/ppermute | solution.py:260
  96.3 0.2 collective-permute-start.14
  96.5 1.6 %collective-permute-start.7 = (bf16[128,896]{1,0:T(8,128)(2,1)S(1)}, bf16[128,896]{1,0:T(8,128)(2,1)S(1)}, u32[]{:S(2)}, u32[]{:S(2)}) collective-permute-start(bf16[128,896]{1,0:T(8,128)(2,1)S(1)} %get-tuple-element.13), channel_id=1, source_target_pairs={{0,12},{12,0},{4,8},{8,4},{1,13},{13,1},{5,9},{9,5},{2,14},{14,2},... | collective-permute-start | bytes 688136 | tf_op jit(solution)/shard_map/ppermute | solution.py:248
  98.2 5.1 %collective-permute-start.15 = (bf16[2,128,256]{2,1,0:T(8,128)(2,1)S(1)}, bf16[2,128,256]{2,1,0:T(8,128)(2,1)S(1)}, u32[]{:S(2)}, u32[]{:S(2)}) collective-permute-start(bf16[2,128,256]{2,1,0:T(8,128)(2,1)S(1)} %pad_maximum_fusion.3), channel_id=1, source_target_pairs={{0,64},{32,96},{64,0},{96,32},{1,65},{33,97},{65,1},{97,33},{2,66}... | collective-permute-start | bytes 393224 | tf_op jit(solution)/shard_map/ppermute | solution.py:272
  103.3 1.0 dynamic-slice_dynamic-update-slice_fusion.15
  104.3 2.3 %collective-permute-start.16 = (bf16[2,128,256]{2,1,0:T(8,128)(2,1)S(1)}, bf16[2,128,256]{2,1,0:T(8,128)(2,1)S(1)}, u32[]{:S(2)}, u32[]{:S(2)}) collective-permute-start(bf16[2,128,256]{2,1,0:T(8,128)(2,1)S(1)} %pad_maximum_fusion.3), channel_id=1, source_target_pairs={{0,96},{32,0},{64,32},{96,64},{1,97},{33,1},{65,33},{97,65},{2,98}... | collective-permute-start | bytes 393224 | tf_op jit(solution)/shard_map/ppermute | solution.py:272
  106.6 1.1 collective-permute-done.15
  107.7 1.6 collective-permute-done.16
  109.3 0.1 collective-permute-start.17
  109.4 1.8 %collective-permute-done.13 = bf16[8,128,448]{1,2,0:T(8,128)(2,1)S(1)} collective-permute-done((bf16[8,128,448]{1,2,0:T(8,128)(2,1)}, bf16[8,128,448]{1,2,0:T(8,128)(2,1)S(1)}, u32[]{:S(2)}, u32[]{:S(2)}) %collective-permute-start.13) | collective-permute-done | bytes 917536 | tf_op jit(solution)/shard_map/ppermute | solution.py:211
  111.2 1.0 dynamic-slice_dynamic-update-slice_fusion.13
  112.3 1.0 dynamic-slice_dynamic-update-slice_fusion.11
  113.3 1.0 dynamic-slice_dynamic-update-slice_fusion.9
  114.4 0.4 convolution_bitcast_fusion
  114.8 0.4 fusion.1
  115.2 0.7 reshape.86
  115.9 7.8 %all-to-all-start.1 = ((bf16[16,28,256]{2,1,0:T(8,128)(2,1)}), bf16[16,28,256]{2,1,0:T(8,128)(2,1)S(1)}, u32[]{:S(2)}, u32[]{:S(2)}) async-start(bf16[16,28,256]{2,1,0:T(8,128)(2,1)} %reshape.86), calls=%async_computation.1 | async-start | bytes 524288 | tf_op jit(solution)/shard_map/all_to_all | solution.py:278
  123.8 0.9 maximum_select_fusion
  124.7 1.1 collective-permute-start.12
  125.7 9.7 %all-to-all-done.1 = bf16[16,28,256]{2,1,0:T(8,128)(2,1)S(1)} async-done(((bf16[16,28,256]{2,1,0:T(8,128)(2,1)}), bf16[16,28,256]{2,1,0:T(8,128)(2,1)S(1)}, u32[]{:S(2)}, u32[]{:S(2)}) %all-to-all-start.1) | async-done | bytes 229408 | tf_op jit(solution)/shard_map/all_to_all | solution.py:278
  135.5 0.9 broadcast_in_dim.19
  136.4 4.0 %all-to-all-start.2 = ((bf16[32,28,256]{2,1,0:T(8,128)(2,1)}), bf16[32,28,256]{2,1,0:T(8,128)(2,1)S(1)}, u32[]{:S(2)}, u32[]{:S(2)}) async-start(bf16[32,28,256]{2,1,0:T(8,128)(2,1)} %broadcast_in_dim.19), calls=%async_computation.2 | async-start | bytes 1048576 | tf_op jit(solution)/shard_map/all_to_all | solution.py:281
  140.4 0.6 maximum_bitcast_fusion
  141.1 0.6 maximum_bitcast_fusion.1
  141.7 14.7 %all-to-all-done.2 = bf16[32,28,256]{2,1,0:T(8,128)(2,1)S(1)} async-done(((bf16[32,28,256]{2,1,0:T(8,128)(2,1)}), bf16[32,28,256]{2,1,0:T(8,128)(2,1)S(1)}, u32[]{:S(2)}, u32[]{:S(2)}) %all-to-all-start.2) | async-done | bytes 458784 | tf_op jit(solution)/shard_map/all_to_all | solution.py:281
  156.5 0.3 copy_convert_fusion
  156.7 0.5 reshape.89
  157.2 0.5 copy.28
  157.7 1.7 %reshape.88 = f32[448,512]{1,0:T(8,128)} reshape(f32[2,8,28,2,2,128]{5,4,3,2,1,0:T(2,128)S(1)} %copy.28) | data formatting | bytes 1835008 | tf_op jit(solution)/shard_map/convert_element_type | solution.py:283
  (56 shorter events, 0.8 us)
Async XLA Ops:
  2.8 4.4 %copy-start.11 = (bf16[1,128,1792]{2,1,0:T(8,128)(2,1)S(1)}, bf16[1,128,1792]{2,1,0:T(8,128)(2,1)}, u32[]{:S(2)}) copy-start(bf16[1,128,1792]{2,1,0:T(8,128)(2,1)} %param.9) | copy-start | bytes 1376260
  2.8 4.4 %copy-start.12 = (bf16[1,128,1792]{2,1,0:T(8,128)(2,1)S(1)}, bf16[1,128,1792]{2,1,0:T(8,128)(2,1)}, u32[]{:S(2)}) copy-start(bf16[1,128,1792]{2,1,0:T(8,128)(2,1)} %param.6) | copy-start | bytes 1376260
  2.8 36.2 %all-to-all-start = ((bf16[8,128,448]{1,2,0:T(8,128)(2,1)}), bf16[8,128,448]{1,2,0:T(8,128)(2,1)}, u32[]{:S(2)}, u32[]{:S(2)}) async-start(bf16[8,128,448]{1,2,0:T(8,128)(2,1)} %bitcast.23), calls=%async_computation | async-start | bytes 1835008 | tf_op jit(solution)/shard_map/all_to_all | solution.py:210
  7.4 3.2 %copy-start.16 = (bf16[1,128,256]{2,1,0:T(8,128)(2,1)S(1)}, bf16[1,128,256]{2,1,0:T(8,128)(2,1)}, u32[]{:S(2)}) copy-start(bf16[1,128,256]{2,1,0:T(8,128)(2,1)} %param.8) | copy-start | bytes 196612
  7.4 3.2 %copy-start.17 = (bf16[1,128,256]{2,1,0:T(8,128)(2,1)S(1)}, bf16[1,128,256]{2,1,0:T(8,128)(2,1)}, u32[]{:S(2)}) copy-start(bf16[1,128,256]{2,1,0:T(8,128)(2,1)} %param.7) | copy-start | bytes 196612
  7.5 41.8 %collective-permute-start = (bf16[256,896]{1,0:T(8,128)(2,1)S(1)}, bf16[256,896]{1,0:T(8,128)(2,1)S(1)}, u32[]{:S(2)}, u32[]{:S(2)}) collective-permute-start(bf16[256,896]{1,0:T(8,128)(2,1)S(1)} %pad_maximum_fusion.1), channel_id=1, source_target_pairs={{0,12},{12,0},{4,8},{8,4},{1,13},{13,1},{5,9},{9,5},{2,14},{14,2},... | collective-permute-start | bytes 1376264 | tf_op jit(solution)/shard_map/ppermute | solution.py:205
  10.6 18.2 %copy-start.10 = (bf16[128,512]{1,0:T(8,128)(2,1)}, bf16[128,512]{1,0:T(8,128)(2,1)S(1)}, u32[]{:S(2)}) copy-start(bf16[128,512]{1,0:T(8,128)(2,1)S(1)} %pad_maximum_fusion.2.a_ref) | copy-start | bytes 393220
  10.6 12.8 %collective-permute-start.1 = (bf16[128,512]{1,0:T(8,128)(2,1)S(1)}, bf16[128,512]{1,0:T(8,128)(2,1)S(1)}, u32[]{:S(2)}, u32[]{:S(2)}) collective-permute-start(bf16[128,512]{1,0:T(8,128)(2,1)S(1)} %pad_maximum_fusion.2.a_ref), channel_id=1, source_target_pairs={{0,1},{1,2},{2,3},{3,0},{4,5},{5,6},{6,7},{7,4},{8,9},{9,10},{10,1... | collective-permute-start | bytes 393224 | tf_op jit(solution)/shard_map/ppermute | solution.py:187
  13.9 12.2 %collective-permute-start.2 = (bf16[128,512]{1,0:T(8,128)(2,1)S(1)}, bf16[128,512]{1,0:T(8,128)(2,1)S(1)}, u32[]{:S(2)}, u32[]{:S(2)}) collective-permute-start(bf16[128,512]{1,0:T(8,128)(2,1)S(1)} %pad_maximum_fusion.2.a_ref), channel_id=1, source_target_pairs={{0,2},{1,3},{2,0},{3,1},{4,6},{5,7},{6,4},{7,5},{8,10},{9,11},{10,... | collective-permute-start | bytes 393224 | tf_op jit(solution)/shard_map/ppermute | solution.py:187
  18.4 10.3 %collective-permute-start.3 = (bf16[128,512]{1,0:T(8,128)(2,1)S(1)}, bf16[128,512]{1,0:T(8,128)(2,1)S(1)}, u32[]{:S(2)}, u32[]{:S(2)}) collective-permute-start(bf16[128,512]{1,0:T(8,128)(2,1)S(1)} %pad_maximum_fusion.2.a_ref), channel_id=1, source_target_pairs={{0,3},{1,0},{2,1},{3,2},{4,7},{5,4},{6,5},{7,6},{8,11},{9,8},{10,9... | collective-permute-start | bytes 393224 | tf_op jit(solution)/shard_map/ppermute | solution.py:187
  23.4 5.3 %copy-start.13 = (bf16[128,512]{1,0:T(8,128)(2,1)}, bf16[128,512]{1,0:T(8,128)(2,1)S(1)}, u32[]{:S(2)}) copy-start(bf16[128,512]{1,0:T(8,128)(2,1)S(1)} %collective-permute-done.1.b_ref) | copy-start | bytes 393220
  26.1 2.7 %copy-start.14 = (bf16[128,512]{1,0:T(8,128)(2,1)}, bf16[128,512]{1,0:T(8,128)(2,1)S(1)}, u32[]{:S(2)}) copy-start(bf16[128,512]{1,0:T(8,128)(2,1)S(1)} %collective-permute-done.2.c_ref) | copy-start | bytes 393220
  28.8 0.7 copy-start.15
  31.4 12.3 %collective-permute-start.4 = (bf16[4,128,256]{2,1,0:T(8,128)(2,1)}, bf16[4,128,256]{2,1,0:T(8,128)(2,1)S(1)}, u32[]{:S(2)}, u32[]{:S(2)}) collective-permute-start(bf16[4,128,256]{2,1,0:T(8,128)(2,1)} %get-tuple-element.11), channel_id=1, source_target_pairs={{0,8},{8,0},{4,12},{1,9},{9,1},{5,13},{2,10},{10,2},{6,14},{3,11},... | collective-permute-start | bytes 786440 | tf_op jit(solution)/shard_map/ppermute | solution.py:191
  34.5 13.3 %collective-permute-start.5 = (bf16[4,128,256]{2,1,0:T(8,128)(2,1)}, bf16[4,128,256]{2,1,0:T(8,128)(2,1)S(1)}, u32[]{:S(2)}, u32[]{:S(2)}) collective-permute-start(bf16[4,128,256]{2,1,0:T(8,128)(2,1)} %get-tuple-element.11), channel_id=1, source_target_pairs={{0,12},{12,0},{4,8},{8,4},{1,13},{13,1},{5,9},{9,5},{2,14},{14,2},... | collective-permute-start | bytes 786440 | tf_op jit(solution)/shard_map/ppermute | solution.py:192
  34.6 14.0 %collective-permute-start.6 = (bf16[4,128,256]{2,1,0:T(8,128)(2,1)}, bf16[4,128,256]{2,1,0:T(8,128)(2,1)S(1)}, u32[]{:S(2)}, u32[]{:S(2)}) collective-permute-start(bf16[4,128,256]{2,1,0:T(8,128)(2,1)} %get-tuple-element.10.kv0_ref), channel_id=1, source_target_pairs={{0,4},{4,0},{8,12},{1,5},{5,1},{9,13},{2,6},{6,2},{10,14},{3,7},{7... | collective-permute-start | bytes 786440 | tf_op jit(solution)/shard_map/ppermute | solution.py:193
  39.0 11.0 %copy-start.9 = (s32[1,2048]{1,0:T(1,128)S(1)}, s32[1,2048]{1,0:T(1,128)}, u32[]{:S(2)}) copy-start(s32[1,2048]{1,0:T(1,128)} %param.11) | copy-start | bytes 24580
  43.7 0.7 copy-start.3
  47.8 0.7 copy-start.5
  48.6 0.7 copy-start.7
  49.3 0.8 copy-start
  50.0 1.0 copy-start.1
  51.1 0.9 copy-start.2
  52.0 0.9 copy-start.4
  53.0 0.9 copy-start.6
  53.9 0.9 copy-start.8
  58.4 18.3 %collective-permute-start.8 = (bf16[4,2,128,256]{3,2,1,0:T(8,128)(2,1)S(1)}, bf16[4,2,128,256]{3,2,1,0:T(8,128)(2,1)S(1)}, u32[]{:S(2)}, u32[]{:S(2)}) collective-permute-start(bf16[4,2,128,256]{3,2,1,0:T(8,128)(2,1)S(1)} %get-tuple-element.15), channel_id=1, source_target_pairs={{0,4},{4,0},{8,12},{12,8},{1,5},{5,1},{9,13},{13,9},{2,6},{6,2},{1... | collective-permute-start | bytes 1572872 | tf_op jit(solution)/shard_map/ppermute | solution.py:255
  76.9 12.5 %collective-permute-start.11 = (bf16[2,128,256]{2,1,0:T(8,128)(2,1)S(1)}, bf16[2,128,256]{2,1,0:T(8,128)(2,1)S(1)}, u32[]{:S(2)}, u32[]{:S(2)}) collective-permute-start(bf16[2,128,256]{2,1,0:T(8,128)(2,1)S(1)} %get-tuple-element.37), channel_id=1, source_target_pairs={{0,3},{1,0},{2,1},{3,2},{4,7},{5,4},{6,5},{7,6},{8,11},{9,8},{10,9... | collective-permute-start | bytes 393224 | tf_op jit(solution)/shard_map/ppermute | solution.py:260
  82.7 13.5 %collective-permute-start.10 = (bf16[2,128,256]{2,1,0:T(8,128)(2,1)S(1)}, bf16[2,128,256]{2,1,0:T(8,128)(2,1)S(1)}, u32[]{:S(2)}, u32[]{:S(2)}) collective-permute-start(bf16[2,128,256]{2,1,0:T(8,128)(2,1)S(1)} %get-tuple-element.38), channel_id=1, source_target_pairs={{0,2},{1,3},{2,0},{3,1},{4,6},{5,7},{6,4},{7,5},{8,10},{9,11},{10,... | collective-permute-start | bytes 393224 | tf_op jit(solution)/shard_map/ppermute | solution.py:260
  83.7 12.5 %collective-permute-start.9 = (bf16[2,128,256]{2,1,0:T(8,128)(2,1)S(1)}, bf16[2,128,256]{2,1,0:T(8,128)(2,1)S(1)}, u32[]{:S(2)}, u32[]{:S(2)}) collective-permute-start(bf16[2,128,256]{2,1,0:T(8,128)(2,1)S(1)} %get-tuple-element.36), channel_id=1, source_target_pairs={{0,1},{1,2},{2,3},{3,0},{4,5},{5,6},{6,7},{7,4},{8,9},{9,10},{10,1... | collective-permute-start | bytes 393224 | tf_op jit(solution)/shard_map/ppermute | solution.py:260
  86.5 24.7 %collective-permute-start.13 = (bf16[8,128,448]{1,2,0:T(8,128)(2,1)}, bf16[8,128,448]{1,2,0:T(8,128)(2,1)S(1)}, u32[]{:S(2)}, u32[]{:S(2)}) collective-permute-start(bf16[8,128,448]{1,2,0:T(8,128)(2,1)} %all-to-all-done), channel_id=1, source_target_pairs={{0,12},{12,0},{4,8},{8,4},{1,13},{13,1},{5,9},{9,5},{2,14},{14,2},... | collective-permute-start | bytes 2752520 | tf_op jit(solution)/shard_map/ppermute | solution.py:211
  96.3 10.2 %collective-permute-start.14 = (bf16[2,128,256]{2,1,0:T(8,128)(2,1)S(1)}, bf16[2,128,256]{2,1,0:T(8,128)(2,1)S(1)}, u32[]{:S(2)}, u32[]{:S(2)}) collective-permute-start(bf16[2,128,256]{2,1,0:T(8,128)(2,1)S(1)} %pad_maximum_fusion.3), channel_id=1, source_target_pairs={{0,32},{32,64},{64,96},{96,0},{1,33},{33,65},{65,97},{97,1},{2,34}... | collective-permute-start | bytes 393224 | tf_op jit(solution)/shard_map/ppermute | solution.py:272
  96.5 27.3 %collective-permute-start.7 = (bf16[128,896]{1,0:T(8,128)(2,1)S(1)}, bf16[128,896]{1,0:T(8,128)(2,1)S(1)}, u32[]{:S(2)}, u32[]{:S(2)}) collective-permute-start(bf16[128,896]{1,0:T(8,128)(2,1)S(1)} %get-tuple-element.13), channel_id=1, source_target_pairs={{0,12},{12,0},{4,8},{8,4},{1,13},{13,1},{5,9},{9,5},{2,14},{14,2},... | collective-permute-start | bytes 688136 | tf_op jit(solution)/shard_map/ppermute | solution.py:248
  98.2 9.5 %collective-permute-start.15 = (bf16[2,128,256]{2,1,0:T(8,128)(2,1)S(1)}, bf16[2,128,256]{2,1,0:T(8,128)(2,1)S(1)}, u32[]{:S(2)}, u32[]{:S(2)}) collective-permute-start(bf16[2,128,256]{2,1,0:T(8,128)(2,1)S(1)} %pad_maximum_fusion.3), channel_id=1, source_target_pairs={{0,64},{32,96},{64,0},{96,32},{1,65},{33,97},{65,1},{97,33},{2,66}... | collective-permute-start | bytes 393224 | tf_op jit(solution)/shard_map/ppermute | solution.py:272
  104.3 5.0 %collective-permute-start.16 = (bf16[2,128,256]{2,1,0:T(8,128)(2,1)S(1)}, bf16[2,128,256]{2,1,0:T(8,128)(2,1)S(1)}, u32[]{:S(2)}, u32[]{:S(2)}) collective-permute-start(bf16[2,128,256]{2,1,0:T(8,128)(2,1)S(1)} %pad_maximum_fusion.3), channel_id=1, source_target_pairs={{0,96},{32,0},{64,32},{96,64},{1,97},{33,1},{65,33},{97,65},{2,98}... | collective-permute-start | bytes 393224 | tf_op jit(solution)/shard_map/ppermute | solution.py:272
  109.3 5.0 %collective-permute-start.17 = (bf16[8,128,256]{2,1,0:T(8,128)(2,1)S(1)}, bf16[8,128,256]{2,1,0:T(8,128)(2,1)S(1)}, u32[]{:S(2)}, u32[]{:S(2)}) collective-permute-start(bf16[8,128,256]{2,1,0:T(8,128)(2,1)S(1)} %constant_dynamic-update-slice_fusion), channel_id=1, source_target_pairs={{0,16},{16,0},{1,17},{17,1},{2,18},{18,2},{3,19},{19,3},{4,20},{20... | collective-permute-start | bytes 1572872 | tf_op jit(solution)/shard_map/ppermute | solution.py:274
  115.9 19.5 %all-to-all-start.1 = ((bf16[16,28,256]{2,1,0:T(8,128)(2,1)}), bf16[16,28,256]{2,1,0:T(8,128)(2,1)S(1)}, u32[]{:S(2)}, u32[]{:S(2)}) async-start(bf16[16,28,256]{2,1,0:T(8,128)(2,1)} %reshape.86), calls=%async_computation.1 | async-start | bytes 524288 | tf_op jit(solution)/shard_map/all_to_all | solution.py:278
  124.7 15.7 %collective-permute-start.12 = (bf16[128,256]{1,0:T(8,128)(2,1)S(1)}, bf16[128,256]{1,0:T(8,128)(2,1)S(1)}, u32[]{:S(2)}, u32[]{:S(2)}) collective-permute-start(bf16[128,256]{1,0:T(8,128)(2,1)S(1)} %bitcast.66), channel_id=1, source_target_pairs={{0,12},{12,0},{4,8},{8,4},{1,13},{13,1},{5,9},{9,5},{2,14},{14,2},... | collective-permute-start | bytes 196616 | tf_op jit(solution)/shard_map/ppermute | solution.py:265
  136.4 20.1 %all-to-all-start.2 = ((bf16[32,28,256]{2,1,0:T(8,128)(2,1)}), bf16[32,28,256]{2,1,0:T(8,128)(2,1)S(1)}, u32[]{:S(2)}, u32[]{:S(2)}) async-start(bf16[32,28,256]{2,1,0:T(8,128)(2,1)} %broadcast_in_dim.19), calls=%async_computation.2 | async-start | bytes 1048576 | tf_op jit(solution)/shard_map/all_to_all | solution.py:281
